TPU v7x, 32 devices: a whole 2x2x4 slice. The times are simulated.
32 devices in a mesh: groups: 2 (over y), feat: 4 (over z), ex: 4 (over x, core).
Axes of the slice: x: 2, y: 2, z: 4, core: 2. Of those that a mesh axis runs over, the one named last changes fastest.
Arguments:
- queries: float32 [512, 65536], P(('groups', 'ex'), 'feat'), parts along dimension 0, may hold values from -6 to 6
- eigenvalues: float32 [65536], P('feat'), may hold values from 0.05 to 5
- train_grads: bfloat16 [16384, 65536], P(('groups', 'ex'), 'feat'), parts along dimension 0, may hold values from -0.0234375 to 0.0234375
- query_index: int32 [512], P(('groups', 'ex')), parts along dimension 0, may hold values from 0 to 63, as said below
- train_index: int32 [16384], P(('groups', 'ex')), parts along dimension 0, may hold values from 0 to 2047, as said below
Outputs:
- scores: float32 [256, 16384], P('feat', ('groups', 'ex')), parts along dimension 1
There are 2 independent parts, one for each index of `groups`. A program takes and returns all parts, laid end to end along the dimension named above; an argument that names none is the same for every part. Nothing has to cross between parts.
Inputs may be any that keep to these rules, and one draw needn't show every extreme that they name: `query_index`: within each aligned block of 64 entries every value appears exactly once. `train_index`: within each aligned block of 2048 entries every value appears exactly once.
All inputs are finite; a program needn't handle non-finite values.
Results may differ from a plain program's by a relative error of at most 0.0029.
Values may be sent and summed in bfloat16 or wider, within the bound.
A program may use at most 192 MiB of HBM per device.

v0:
```python
import jax
import jax.numpy as jnp
from jax import lax
from jax.sharding import PartitionSpec as P

damping = 0.05


def from_behind(block, axis, distance):
    devices = range(lax.axis_size(axis))
    route = [((i - distance) % len(devices), i) for i in devices]
    return lax.ppermute(block, axis, route)


def products(left, train_grads):
    return lax.dot_general(
        left, train_grads, (((1,), (1,)), ((), ())), preferred_element_type=jnp.float32
    )


def local(queries, eigenvalues, train_grads, query_index, train_index):
    block_size = queries.shape[0]
    local_rows = train_grads.shape[0]
    cycle_size = lax.axis_size("ex")
    total_queries = block_size * cycle_size
    selected = jnp.take(queries, query_index, axis=0)
    scaled = (selected / (eigenvalues + damping)[None, :]).astype(jnp.bfloat16)
    partial_value = jnp.zeros((total_queries, local_rows), jnp.float32)
    resident = scaled
    position = lax.axis_index("ex")
    for turn in range(cycle_size):
        block_id = (position - turn) % cycle_size
        partial_value = lax.dynamic_update_slice_in_dim(
            partial_value, products(resident, train_grads), block_id * block_size, 0
        )
        if turn + 1 < cycle_size:
            resident = from_behind(resident, "ex", 1)
    summed = lax.psum_scatter(partial_value, "feat", scatter_dimension=0, tiled=True)
    return jnp.take(summed, train_index, axis=1)


def solution(mesh):
    return jax.shard_map(
        local,
        mesh=mesh,
        in_specs=(
            P(("groups", "ex"), "feat"),
            P("feat"),
            P(("groups", "ex"), "feat"),
            P(("groups", "ex")),
            P(("groups", "ex")),
        ),
        out_specs=P("feat", ("groups", "ex")),
        check_vma=False,
    )
```

profile of v0, /device:TPU:0, one launch (start us, length us, event | category | flops | bytes accessed | tf_op | source)
XLA Modules:
  0.0 222.8 jit_solution(11442987945450967970)
XLA Ops:
  6.5 0.0 reduce-scatter.4.cloned.1.call-start
  6.5 0.7 compare_select_fusion.1
  7.2 0.7 compare_and_fusion.1
  7.9 0.8 broadcast_add_fusion
  8.7 7.6 %gather_fusion = f32[64,16384]{1,0:T(8,128)} fusion(f32[64,16384]{1,0:T(8,128)} %param.5, s32[1024]{0:T(1024)S(1)} %pad_clamp_fusion), kind=kCustom, calls=%fused_computation | custom fusion | bytes 8388864 | tf_op jit(solution)/shard_map/jit(_take)/gather | solution.py:26
  16.3 2.6 %divide_convert_fusion = bf16[64,16384]{1,0:T(8,128)(2,1)S(1)} fusion(f32[64,16384]{1,0:T(8,128)} %gather_fusion, f32[16384]{0:T(1024)S(1)} %broadcast_add_fusion, pred[64]{0:T(512)(128)(4,1)S(1)} %compare_and_fusion.1), kind=kLoop, calls=%fused_computation.2 | loop fusion | flops 3145728 | bytes 6357056 | tf_op jit(solution)/shard_map/convert_element_type | solution.py:27
  18.9 0.5 collective-permute-start
  19.4 26.1 %fusion.1 = f32[64,2048]{0,1:T(8,128)S(1)} fusion(bf16[64,16384]{1,0:T(8,128)(2,1)S(1)} %divide_convert_fusion, bf16[2048,16384]{1,0:T(8,128)(2,1)} %param.7), kind=kOutput, calls=%fused_computation.11 | convolution fusion | flops 4294967296 | bytes 69730304 | tf_op jit(solution)/shard_map/dot_general | solution.py:16
  45.5 1.5 broadcast_in_dim.29
  47.0 5.9 %dynamic_update_slice.12 = f32[256,2048]{0,1:T(8,128)} dynamic-update-slice(f32[256,2048]{0,1:T(8,128)} %broadcast_in_dim.29, f32[64,2048]{0,1:T(8,128)S(1)} %fusion.1, s32[]{:T(128)S(6)} %select_n.53, s32[]{:T(128)} %constant.60.clone.1) | dynamic-update-slice | bytes 1048580 | tf_op jit(solution)/shard_map/dynamic_update_slice | solution.py:33
  52.9 0.0 collective-permute-done
  52.9 0.0 copy-start
  52.9 3.3 %collective-permute-start.1 = (bf16[64,16384]{1,0:T(8,128)(2,1)}, bf16[64,16384]{1,0:T(8,128)(2,1)}, u32[]{:S(2)}, u32[]{:S(2)}) collective-permute-start(bf16[64,16384]{1,0:T(8,128)(2,1)} %collective-permute-done), channel_id=1, source_target_pairs={{3,0},{0,1},{1,2},{2,3},{7,4},{4,5},{5,6},{6,7},{11,8},{8,9},{9,10... | collective-permute-start | bytes 6291464 | tf_op jit(solution)/shard_map/ppermute | solution.py:12
  56.2 26.7 %fusion.2 = f32[64,2048]{0,1:T(8,128)S(1)} fusion(bf16[64,16384]{1,0:T(8,128)(2,1)} %collective-permute-done, bf16[2048,16384]{1,0:T(8,128)(2,1)} %param.7), kind=kOutput, calls=%fused_computation.12 | convolution fusion | flops 4294967296 | bytes 69730304 | tf_op jit(solution)/shard_map/dot_general | solution.py:16
  82.9 0.0 copy-done
  82.9 6.1 %dynamic_update_slice.13 = f32[256,2048]{0,1:T(8,128)S(1)} dynamic-update-slice(f32[256,2048]{0,1:T(8,128)S(1)} %copy-done, f32[64,2048]{0,1:T(8,128)S(1)} %fusion.2, s32[]{:T(128)S(6)} %select_n.55, s32[]{:T(128)} %constant.60.clone.1) | dynamic-update-slice | bytes 1048580 | tf_op jit(solution)/shard_map/dynamic_update_slice | solution.py:33
  89.0 0.0 collective-permute-done.1
  89.0 2.3 %collective-permute-start.2 = (bf16[64,16384]{1,0:T(8,128)(2,1)}, bf16[64,16384]{1,0:T(8,128)(2,1)}, u32[]{:S(2)}, u32[]{:S(2)}) collective-permute-start(bf16[64,16384]{1,0:T(8,128)(2,1)} %collective-permute-done.1), channel_id=1, source_target_pairs={{3,0},{0,1},{1,2},{2,3},{7,4},{4,5},{5,6},{6,7},{11,8},{8,9},{9,10... | collective-permute-start | bytes 6291464 | tf_op jit(solution)/shard_map/ppermute | solution.py:12
  91.3 26.7 %fusion.3 = f32[64,2048]{0,1:T(8,128)S(1)} fusion(bf16[64,16384]{1,0:T(8,128)(2,1)} %collective-permute-done.1, bf16[2048,16384]{1,0:T(8,128)(2,1)} %param.7), kind=kOutput, calls=%fused_computation.13 | convolution fusion | flops 4294967296 | bytes 69730304 | tf_op jit(solution)/shard_map/dot_general | solution.py:16
  118.0 4.5 %dynamic_update_slice.14 = f32[256,2048]{0,1:T(8,128)S(1)} dynamic-update-slice(f32[256,2048]{0,1:T(8,128)S(1)} %dynamic_update_slice.13, f32[64,2048]{0,1:T(8,128)S(1)} %fusion.3, s32[]{:T(128)S(6)} %select_n.57, s32[]{:T(128)} %constant.60.clone.1) | dynamic-update-slice | bytes 1048580 | tf_op jit(solution)/shard_map/dynamic_update_slice | solution.py:33
  122.6 0.0 collective-permute-done.2
  122.6 26.7 %fusion.4 = f32[64,2048]{0,1:T(8,128)S(1)} fusion(bf16[64,16384]{1,0:T(8,128)(2,1)} %collective-permute-done.2, bf16[2048,16384]{1,0:T(8,128)(2,1)} %param.7), kind=kOutput, calls=%fused_computation.14 | convolution fusion | flops 4294967296 | bytes 69730304 | tf_op jit(solution)/shard_map/dot_general | solution.py:16
  149.3 0.0 copy-start.1
  149.3 9.5 %dynamic_update_slice.15 = f32[256,2048]{0,1:T(8,128)S(1)} dynamic-update-slice(f32[256,2048]{0,1:T(8,128)S(1)} %dynamic_update_slice.14, f32[64,2048]{0,1:T(8,128)S(1)} %fusion.4, s32[]{:T(128)S(6)} %select_n.59, s32[]{:T(128)} %constant.60.clone.1) | dynamic-update-slice | bytes 1048580 | tf_op jit(solution)/shard_map/dynamic_update_slice | solution.py:33
  158.8 1.9 copy.20
  160.7 0.0 reduce-scatter.4.cloned.1.call-update
  160.7 0.0 copy-done.1
  160.8 46.9 %reduce-scatter.4.cloned.1.call-done = f32[64,2048]{1,0:T(8,128)} async-done(((f32[256,2048]{1,0:T(8,128)}), f32[64,2048]{1,0:T(8,128)}) %reduce-scatter.4.cloned.1.call-update) | async-done | bytes 524304
  207.7 1.4 copy.21
  209.1 5.5 %gather_fusion.1 = f32[2048,64]{1,0:T(8,128)S(1)} fusion(f32[64,2048]{0,1:T(8,128)S(1)} %copy.21, s32[2048]{0:T(1024)S(1)} %fusion), kind=kCustom, calls=%fused_computation.1 | custom fusion | bytes 1056768 | tf_op jit(solution)/shard_map/jit(_take)/gather | solution.py:39
  214.5 0.3 select_bitcast_fusion
  214.9 1.1 copy.15
  (3 shorter events, 0.0 us)
Async XLA Ops:
  6.5 201.1 %reduce-scatter.4.cloned.1.call-start = ((), (), s32[]{:S(2)}) async-start(), calls=%async_computation.1 | async-start | bytes 2621440
  18.9 33.9 %collective-permute-start = (bf16[64,16384]{1,0:T(8,128)(2,1)S(1)}, bf16[64,16384]{1,0:T(8,128)(2,1)}, u32[]{:S(2)}, u32[]{:S(2)}) collective-permute-start(bf16[64,16384]{1,0:T(8,128)(2,1)S(1)} %divide_convert_fusion), channel_id=1, source_target_pairs={{3,0},{0,1},{1,2},{2,3},{7,4},{4,5},{5,6},{6,7},{11,8},{8,9},{9,10... | collective-permute-start | bytes 6291464 | tf_op jit(solution)/shard_map/ppermute | solution.py:12
  52.9 30.0 %copy-start = (f32[256,2048]{0,1:T(8,128)S(1)}, f32[256,2048]{0,1:T(8,128)}, u32[]{:S(2)}) copy-start(f32[256,2048]{0,1:T(8,128)} %dynamic_update_slice.12) | copy-start | bytes 6291460
  52.9 36.1 %collective-permute-start.1 = (bf16[64,16384]{1,0:T(8,128)(2,1)}, bf16[64,16384]{1,0:T(8,128)(2,1)}, u32[]{:S(2)}, u32[]{:S(2)}) collective-permute-start(bf16[64,16384]{1,0:T(8,128)(2,1)} %collective-permute-done), channel_id=1, source_target_pairs={{3,0},{0,1},{1,2},{2,3},{7,4},{4,5},{5,6},{6,7},{11,8},{8,9},{9,10... | collective-permute-start | bytes 6291464 | tf_op jit(solution)/shard_map/ppermute | solution.py:12
  89.0 33.6 %collective-permute-start.2 = (bf16[64,16384]{1,0:T(8,128)(2,1)}, bf16[64,16384]{1,0:T(8,128)(2,1)}, u32[]{:S(2)}, u32[]{:S(2)}) collective-permute-start(bf16[64,16384]{1,0:T(8,128)(2,1)} %collective-permute-done.1), channel_id=1, source_target_pairs={{3,0},{0,1},{1,2},{2,3},{7,4},{4,5},{5,6},{6,7},{11,8},{8,9},{9,10... | collective-permute-start | bytes 6291464 | tf_op jit(solution)/shard_map/ppermute | solution.py:12
  149.3 11.5 %copy-start.1 = (s32[2048]{0:T(1024)S(1)}, s32[2048]{0:T(1024)}, u32[]{:S(2)}) copy-start(s32[2048]{0:T(1024)} %param.9) | copy-start | bytes 24580
Sparse Core Ops, SparseCore 0:
  160.9 46.7 reduce-scatter.3
where the time goes:
time: 224 us; the launch traced here: 223 us
  matrix products  106 us (47%)
  waiting for transfers between devices  46.9 us (21%)
  local copies, waits for them, and re-layouts  44.9 us (20%)
  between operations  13.5 us (6%)
  starting transfers between devices  6.14 us (3%)
  other arithmetic  5.14 us (2%)
    dot_general x4, matrix products, products(): lax.dot_general(left, train_grads, (((1,), (1,)), ((), ())), preferred_el...  106 us
    unnamed x2, waiting for transfers between devices  46.9 us
    dynamic_update_slice x4, local copies, waits for them, and re-layouts, local(): lax.dynamic_update_slice_in_dim(partial_value, products(resident, train_g...  26 us
    gather x1, local copies, waits for them, and re-layouts, local(): selected = jnp.take(queries, query_index, axis=0)  7.6 us
    ppermute x3, starting transfers between devices, from_behind(): return lax.ppermute(block, axis, route)  6.14 us
    gather x1, local copies, waits for them, and re-layouts, local(): return jnp.take(summed, train_index, axis=1)  5.47 us
  transfers between devices with their start and end apart: 4, of which 1 were waited for; matrix products, arithmetic and copies ran while one was open for 44% of the time, Pallas kernels for 0%

commit v1 on v0

--- a/solution.py
+++ b/solution.py
@@ -1,6 +1,8 @@
 import jax
 import jax.numpy as jnp
 from jax import lax
+from jax.experimental import pallas as pl
+from jax.experimental.pallas import tpu as pltpu
 from jax.sharding import PartitionSpec as P
 
 damping = 0.05
@@ -18,7 +20,7 @@
     )
 
 
-def local(queries, eigenvalues, train_grads, query_index, train_index):
+def ring_local(queries, eigenvalues, train_grads, query_index, train_index):
     block_size = queries.shape[0]
     local_rows = train_grads.shape[0]
     cycle_size = lax.axis_size("ex")
@@ -39,6 +41,244 @@
     return jnp.take(summed, train_index, axis=1)
 
 
+WIDTH = 1024
+WINDOW = 6
+KEPT = 4
+SLOTS = 3
+HALVES = 2
+MESH = pl.DeviceIdType.MESH
+
+
+def kernel(
+    queries, eigenvalues, query_index, train_index, train, out,
+    stack, acc, order, kept, ring, outgoing, incoming,
+    kept_sem, ring_sem, far_send, far_recv, fwd_send, fwd_recv,
+    sib_send, sib_recv, sum_send, sum_recv,
+):
+    me = lax.axis_index("ex")
+    z = lax.axis_index("feat")
+    sib = me + 1 - 2 * lax.rem(me, 2)
+    far = lax.rem(me + 2, 4)
+    far_sib = lax.rem(sib + 2, 4)
+    rows = queries.shape[0]
+    half = rows // HALVES
+    chunks = queries.shape[1] // WIDTH
+    total = HALVES * chunks
+    local_rows = train.shape[0]
+    feats = incoming.shape[0]
+
+    barrier = pltpu.get_barrier_semaphore()
+    pl.semaphore_signal(barrier, inc=1, device_id={"ex": sib}, device_id_type=MESH)
+    pl.semaphore_signal(barrier, inc=1, device_id={"ex": far}, device_id_type=MESH)
+    for d in range(1, feats):
+        pl.semaphore_signal(barrier, inc=1, device_id={"feat": lax.rem(z + d, feats)}, device_id_type=MESH)
+
+    def columns(k):
+        return pl.ds(pl.multiple_of(k * WIDTH, WIDTH), WIDTH)
+
+    def place(owner, j):
+        return stack.at[j // chunks, pl.ds(pl.multiple_of(owner * half, half), half), columns(j % chunks)]
+
+    def to_far(j):
+        return pltpu.make_async_remote_copy(
+            place(me, j), place(me, j), far_send.at[j], far_recv.at[j], device_id={"ex": far}, device_id_type=MESH)
+
+    def from_far(j):
+        return pltpu.make_async_remote_copy(
+            place(far, j), place(far, j), far_send.at[j], far_recv.at[j], device_id={"ex": far}, device_id_type=MESH)
+
+    def to_sib(j):
+        return pltpu.make_async_remote_copy(
+            place(me, j), place(me, j), sib_send.at[j], sib_recv.at[j], device_id={"ex": sib}, device_id_type=MESH)
+
+    def from_sib(j):
+        return pltpu.make_async_remote_copy(
+            place(sib, j), place(sib, j), sib_send.at[j], sib_recv.at[j], device_id={"ex": sib}, device_id_type=MESH)
+
+    def forward(j):
+        return pltpu.make_async_remote_copy(
+            place(far, j), place(far, j), fwd_send.at[j], fwd_recv.at[j], device_id={"ex": sib}, device_id_type=MESH)
+
+    def forwarded(j):
+        return pltpu.make_async_remote_copy(
+            place(far_sib, j), place(far_sib, j), fwd_send.at[j], fwd_recv.at[j], device_id={"ex": sib}, device_id_type=MESH)
+
+    streamed = chunks - KEPT
+
+    def keep(k):
+        return pltpu.make_async_copy(train.at[:, columns(k)], kept.at[k], kept_sem.at[k])
+
+    def stream(s):
+        return pltpu.make_async_copy(
+            train.at[:, columns(KEPT + lax.rem(s, streamed))], ring.at[lax.rem(s, SLOTS)], ring_sem.at[lax.rem(s, SLOTS)])
+
+    for k in range(KEPT):
+        keep(k).start()
+    for s in range(SLOTS):
+        stream(jnp.int32(s)).start()
+
+    lanes = lax.broadcasted_iota(jnp.int32, (rows, rows), 1)
+    pick = (query_index[...] == lanes).astype(jnp.float32).astype(jnp.bfloat16)
+
+    def scale(k):
+        inverse = 1.0 / (eigenvalues[:, columns(k)] + damping)
+        scaled = (queries[:, columns(k)] * inverse).astype(jnp.bfloat16)
+        selected = jnp.dot(pick, scaled, preferred_element_type=jnp.float32).astype(jnp.bfloat16)
+        mine = pl.ds(pl.multiple_of(me * half, half), half)
+        for h in range(HALVES):
+            stack[h, mine, columns(k)] = selected[h * half:(h + 1) * half]
+
+    scale(0)
+    pl.semaphore_wait(barrier, feats + 1)
+
+    def first(k, carry):
+        to_far(k).start()
+        to_sib(k).start()
+        to_sib(chunks + k).start()
+        scale(k + 1)
+        return carry
+
+    def later(k, carry):
+        scale(k)
+        to_sib(k).start()
+        to_sib(chunks + k).start()
+        return carry
+
+    lax.fori_loop(0, WINDOW - 1, first, 0)
+    to_far(WINDOW - 1).start()
+    to_sib(WINDOW - 1).start()
+    to_sib(chunks + WINDOW - 1).start()
+    lax.fori_loop(WINDOW, chunks, later, 0)
+
+    from_far(0).wait_recv()
+    forward(0).start()
+    to_far(WINDOW).start()
+    acc[...] = jnp.zeros_like(acc)
+
+    tile = 256
+    def build(i, carry):
+        at = pl.ds(pl.multiple_of(i * tile, tile), tile)
+        positions = lax.broadcasted_iota(jnp.int32, (tile, local_rows), 0) + i * tile
+        order[at, :] = (train_index[...] == positions).astype(jnp.float32).astype(jnp.bfloat16)
+        return carry
+
+    lax.fori_loop(0, local_rows // tile, build, 0)
+
+    def ready(j):
+        @pl.when(j + 1 < total)
+        def _():
+            from_far(j + 1).wait_recv()
+            forward(j + 1).start()
+
+        @pl.when(j + 1 + WINDOW < total)
+        def _():
+            to_far(j + 1 + WINDOW).start()
+
+        from_sib(j).wait_recv()
+        forwarded(j).wait_recv()
+
+    def multiply(h, k, block):
+        acc[h] += lax.dot_general(
+            stack[h, :, columns(k)], block[...], (((1,), (1,)), ((), ())),
+            preferred_element_type=jnp.float32)
+
+    def sums(h, d):
+        to = lax.rem(z + d, feats)
+        n = h * (feats - 1) + d - 1
+        return pltpu.make_async_remote_copy(
+            outgoing.at[h, pl.ds(pl.multiple_of(to * half, half), half), :], incoming.at[z, h],
+            sum_send.at[n], sum_recv.at[n], device_id={"feat": to}, device_id_type=MESH)
+
+    def arriving(h, d):
+        n = h * (feats - 1) + d - 1
+        return pltpu.make_async_remote_copy(
+            incoming.at[lax.rem(z - d + feats, feats), h], incoming.at[lax.rem(z - d + feats, feats), h],
+            sum_send.at[n], sum_recv.at[n], device_id={"feat": lax.rem(z + d, feats)}, device_id_type=MESH)
+
+    for h in range(HALVES):
+        def from_kept(k, carry, h=h):
+            ready(h * chunks + k)
+            if h == 0:
+                keep(k).wait()
+            multiply(h, k, kept.at[k])
+            return carry
+
+        def from_ring(k, carry, h=h):
+            s = h * streamed + k - KEPT
+            ready(h * chunks + k)
+            stream(s).wait()
+            multiply(h, k, ring.at[lax.rem(s, SLOTS)])
+
+            @pl.when(s + SLOTS < HALVES * streamed)
+            def _():
+                stream(s + SLOTS).start()
+            return carry
+
+        lax.fori_loop(0, KEPT, from_kept, 0)
+        lax.fori_loop(KEPT, chunks, from_ring, 0)
+
+        def arrange(i, carry, h=h):
+            at = pl.ds(pl.multiple_of(i * tile, tile), tile)
+            outgoing[h, :, at] = jnp.dot(
+                acc[h].astype(jnp.bfloat16), order[:, at],
+                preferred_element_type=jnp.float32).astype(jnp.bfloat16)
+            return carry
+
+        lax.fori_loop(0, local_rows // tile, arrange, 0)
+        for d in range(1, feats):
+            sums(h, d).start()
+
+    for h in range(HALVES):
+        summed = outgoing[h, pl.ds(pl.multiple_of(z * half, half), half), :].astype(jnp.float32)
+        for d in range(1, feats):
+            arriving(h, d).wait_recv()
+            summed += incoming[lax.rem(z - d + feats, feats), h].astype(jnp.float32)
+        out[h * half:(h + 1) * half, :] = summed
+
+    def drain(j, carry):
+        to_far(j).wait_send()
+        to_sib(j).wait_send()
+        forward(j).wait_send()
+        return carry
+
+    lax.fori_loop(0, total, drain, 0)
+    for h in range(HALVES):
+        for d in range(1, feats):
+            sums(h, d).wait_send()
+
+
+def local(queries, eigenvalues, train_grads, query_index, train_index):
+    rows, features = queries.shape
+    feats = lax.axis_size("feat")
+    local_rows = train_grads.shape[0]
+    if lax.axis_size("ex") != 4 or feats != 4 or features < 8 * WIDTH:
+        return ring_local(queries, eigenvalues, train_grads, query_index, train_index)
+    half = rows // HALVES
+    total = HALVES * (features // WIDTH)
+    vmem = pl.BlockSpec(memory_space=pltpu.VMEM)
+    links = HALVES * (feats - 1)
+    return pl.pallas_call(
+        kernel,
+        out_shape=jax.ShapeDtypeStruct((rows, local_rows), jnp.float32),
+        in_specs=[vmem, vmem, vmem, vmem, pl.BlockSpec(memory_space=pl.ANY)],
+        out_specs=vmem,
+        scratch_shapes=[
+            pltpu.VMEM((HALVES, 4 * half, features), jnp.bfloat16),
+            pltpu.VMEM((HALVES, 4 * half, local_rows), jnp.float32),
+            pltpu.VMEM((local_rows, local_rows), jnp.bfloat16),
+            pltpu.VMEM((KEPT, local_rows, WIDTH), jnp.bfloat16),
+            pltpu.VMEM((SLOTS, local_rows, WIDTH), jnp.bfloat16),
+            pltpu.VMEM((HALVES, 4 * half, local_rows), jnp.bfloat16),
+            pltpu.VMEM((feats, HALVES, half, local_rows), jnp.bfloat16),
+            pltpu.SemaphoreType.DMA((KEPT,)),
+            pltpu.SemaphoreType.DMA((SLOTS,)),
+        ] + [pltpu.SemaphoreType.DMA((total,))] * 6 + [pltpu.SemaphoreType.DMA((links,))] * 2,
+        compiler_params=pltpu.CompilerParams(
+            collective_id=0, has_side_effects=True, vmem_limit_bytes=60 * 1024 * 1024),
+        name="scores",
+    )(queries, eigenvalues.reshape(1, -1), query_index.reshape(-1, 1), train_index.reshape(1, -1), train_grads)
+
+
 def solution(mesh):
     return jax.shard_map(
         local,

time: 224 us -> 84.4 us (0.38)
  matrix products: 106 us -> 0 us
  Pallas kernels: 0 us -> 80.6 us
  waiting for transfers between devices: 46.9 us -> 0 us
  local copies, waits for them, and re-layouts: 44.9 us -> 3.23 us
  between operations: 13.5 us -> 0.01 us
  starting transfers between devices: 6.14 us -> 0 us
  other arithmetic: 5.14 us -> 0 us
    dot_general x4 -> x0, matrix products: 106 us -> none  [products(): lax.dot_general(left, train_grads, (((1,), (1,)), ((), ())), preferred_el...]
    pallas_call x0 -> x1, Pallas kernels: none -> 80.6 us  [local(): pl.pallas_call(kernel, out_shape=jax.ShapeDtypeStruct((rows, local_rows),...]
    unnamed x2 -> x0, waiting for transfers between devices: 46.9 us -> none
    dynamic_update_slice x4 -> x0, local copies, waits for them, and re-layouts: 26 us -> none  [local(): lax.dynamic_update_slice_in_dim(partial_value, products(resident, train_g...]
    gather x2 -> x0, local copies, waits for them, and re-layouts: 13.1 us -> none  [the longest x1 7.6 us: local(): selected = jnp.take(queries, query_index, axis=0)]
    ppermute x3 -> x0, starting transfers between devices: 6.14 us -> none  [from_behind(): return lax.ppermute(block, axis, route)]
    convert_element_type x1 -> x0, other arithmetic: 2.62 us -> none  [local(): scaled = (selected / (eigenvalues + damping)[None, :]).astype(jnp.bfloat16)]
  transfers between devices with their start and end apart: 4 -> 0, of which waited for: 1 -> 0; matrix products, arithmetic and copies ran while one was open for 44% -> 0% of each run, Pallas kernels for 0% -> 0%
where the time goes in v1:
time: 84.4 us; the launch traced here: 83.9 us
  Pallas kernels  80.6 us (95%)
  local copies, waits for them, and re-layouts  3.23 us (4%)
    pallas_call x1, Pallas kernels, local(): pl.pallas_call(kernel, out_shape=jax.ShapeDtypeStruct((rows, local_rows),...  80.6 us
    unnamed x1, local copies, waits for them, and re-layouts  1.87 us

profile of v1, /device:TPU:0, one launch (start us, length us, event | category | flops | bytes accessed | tf_op | source)
XLA Modules:
  0.0 83.9 jit_solution(17330758646327887744)
XLA Ops:
  0.0 1.4 %copy.6.query_index = s32[64,1]{1,0:T(8,128)} copy(s32[64,1]{0,1:T(1,128)} %bitcast.5) | data formatting | bytes 512 | tf_op jit(solution)/shard_map/reshape | solution.py:279
  1.4 80.6 %scores.1 = f32[64,2048]{1,0:T(8,128)} custom-call(f32[64,16384]{1,0:T(8,128)} %queries.1, f32[1,16384]{1,0:T(1,128)} %bitcast.3, s32[64,1]{1,0:T(8,128)} %copy.6.query_index, s32[1,2048]{1,0:T(1,128)} %bitcast.4, bf16[2048,16384]{1,0:T(8,128)(2,1)} %train.1), custom_call_target="tpu_custom_call" | custom-call | tf_op jit(solution)/shard_map/scores/pallas_call | solution.py:260
  82.0 1.9 %copy.8 = f32[64,2048]{1,0:T(8,128)} copy(f32[64,2048]{1,0:T(8,128)} %scores.1) | data formatting | bytes 1048576

commit v2 on v1

--- a/solution.py
+++ b/solution.py
@@ -42,18 +42,19 @@
 
 
 WIDTH = 1024
-WINDOW = 6
+WINDOW = 12
 KEPT = 4
 SLOTS = 3
 HALVES = 2
+PIECES = 4
 MESH = pl.DeviceIdType.MESH
 
 
 def kernel(
-    queries, eigenvalues, query_index, train_index, train, out,
-    stack, acc, order, kept, ring, outgoing, incoming,
+    eigenvalues, query_index, train_index, queries_hbm, train, out,
+    queries, stack, acc, order, kept, ring, outgoing, incoming,
     kept_sem, ring_sem, far_send, far_recv, fwd_send, fwd_recv,
-    sib_send, sib_recv, sum_send, sum_recv,
+    sib_send, sib_recv, query_sem, sum_send, sum_recv,
 ):
     me = lax.axis_index("ex")
     z = lax.axis_index("feat")
@@ -112,18 +113,26 @@
         return pltpu.make_async_copy(
             train.at[:, columns(KEPT + lax.rem(s, streamed))], ring.at[lax.rem(s, SLOTS)], ring_sem.at[lax.rem(s, SLOTS)])
 
+    def load(k):
+        return pltpu.make_async_copy(queries_hbm.at[:, columns(k)], queries.at[:, columns(k)], query_sem.at[k])
+
+    for k in range(chunks):
+        load(k).start()
+    for k in range(chunks):
+        load(k).wait()
     for k in range(KEPT):
         keep(k).start()
     for s in range(SLOTS):
         stream(jnp.int32(s)).start()
 
-    lanes = lax.broadcasted_iota(jnp.int32, (rows, rows), 1)
-    pick = (query_index[...] == lanes).astype(jnp.float32).astype(jnp.bfloat16)
+    sources = lax.broadcasted_iota(jnp.int32, (rows, rows), 0)
+    pick = (query_index[...] == sources).astype(jnp.float32).astype(jnp.bfloat16)
 
     def scale(k):
         inverse = 1.0 / (eigenvalues[:, columns(k)] + damping)
         scaled = (queries[:, columns(k)] * inverse).astype(jnp.bfloat16)
-        selected = jnp.dot(pick, scaled, preferred_element_type=jnp.float32).astype(jnp.bfloat16)
+        selected = lax.dot_general(
+            pick, scaled, (((0,), (0,)), ((), ())), preferred_element_type=jnp.float32).astype(jnp.bfloat16)
         mine = pl.ds(pl.multiple_of(me * half, half), half)
         for h in range(HALVES):
             stack[h, mine, columns(k)] = selected[h * half:(h + 1) * half]
@@ -179,21 +188,33 @@
 
     def multiply(h, k, block):
         acc[h] += lax.dot_general(
-            stack[h, :, columns(k)], block[...], (((1,), (1,)), ((), ())),
+            block[...], stack[h, :, columns(k)], (((1,), (1,)), ((), ())),
             preferred_element_type=jnp.float32)
 
-    def sums(h, d):
-        to = lax.rem(z + d, feats)
-        n = h * (feats - 1) + d - 1
-        return pltpu.make_async_remote_copy(
-            outgoing.at[h, pl.ds(pl.multiple_of(to * half, half), half), :], incoming.at[z, h],
+    part = local_rows // PIECES
+
+    def piece(i):
+        return pl.ds(pl.multiple_of(i * part, part), part)
+
+    def number(h, d, i):
+        return (h * (feats - 1) + d - 1) * PIECES + i
+
+    def partner(d):
+        return {1: z + 1 - 2 * lax.rem(z, 2), 2: lax.rem(z + 2, 4), 3: 3 - z}[d]
+
+    def sums(h, d, i):
+        to = partner(d)
+        n = number(h, d, i)
+        return pltpu.make_async_remote_copy(
+            outgoing.at[h, pl.ds(pl.multiple_of(to * half, half), half), piece(i)], incoming.at[z, h, :, piece(i)],
             sum_send.at[n], sum_recv.at[n], device_id={"feat": to}, device_id_type=MESH)
 
-    def arriving(h, d):
-        n = h * (feats - 1) + d - 1
-        return pltpu.make_async_remote_copy(
-            incoming.at[lax.rem(z - d + feats, feats), h], incoming.at[lax.rem(z - d + feats, feats), h],
-            sum_send.at[n], sum_recv.at[n], device_id={"feat": lax.rem(z + d, feats)}, device_id_type=MESH)
+    def arriving(h, d, i):
+        n = number(h, d, i)
+        source = partner(d)
+        return pltpu.make_async_remote_copy(
+            incoming.at[source, h, :, piece(i)], incoming.at[source, h, :, piece(i)],
+            sum_send.at[n], sum_recv.at[n], device_id={"feat": source}, device_id_type=MESH)
 
     for h in range(HALVES):
         def from_kept(k, carry, h=h):
@@ -217,23 +238,27 @@
         lax.fori_loop(0, KEPT, from_kept, 0)
         lax.fori_loop(KEPT, chunks, from_ring, 0)
 
+        turned = acc[h].T.astype(jnp.bfloat16)
+
         def arrange(i, carry, h=h):
-            at = pl.ds(pl.multiple_of(i * tile, tile), tile)
-            outgoing[h, :, at] = jnp.dot(
-                acc[h].astype(jnp.bfloat16), order[:, at],
-                preferred_element_type=jnp.float32).astype(jnp.bfloat16)
+            outgoing[h, :, piece(i)] = jnp.dot(
+                turned, order[:, piece(i)], preferred_element_type=jnp.float32).astype(jnp.bfloat16)
+            for d in (2, 3, 1):
+                sums(h, d, i).start()
             return carry
 
-        lax.fori_loop(0, local_rows // tile, arrange, 0)
-        for d in range(1, feats):
-            sums(h, d).start()
+        lax.fori_loop(0, PIECES, arrange, 0)
 
     for h in range(HALVES):
-        summed = outgoing[h, pl.ds(pl.multiple_of(z * half, half), half), :].astype(jnp.float32)
-        for d in range(1, feats):
-            arriving(h, d).wait_recv()
-            summed += incoming[lax.rem(z - d + feats, feats), h].astype(jnp.float32)
-        out[h * half:(h + 1) * half, :] = summed
+        def gather(i, carry, h=h):
+            summed = outgoing[h, pl.ds(pl.multiple_of(z * half, half), half), piece(i)].astype(jnp.float32)
+            for d in (1, 2, 3):
+                arriving(h, d, i).wait_recv()
+                summed += incoming[partner(d), h, :, piece(i)].astype(jnp.float32)
+            out[h * half:(h + 1) * half, piece(i)] = summed
+            return carry
+
+        lax.fori_loop(0, PIECES, gather, 0)
 
     def drain(j, carry):
         to_far(j).wait_send()
@@ -244,7 +269,8 @@
     lax.fori_loop(0, total, drain, 0)
     for h in range(HALVES):
         for d in range(1, feats):
-            sums(h, d).wait_send()
+            for i in range(PIECES):
+                sums(h, d, i).wait_send()
 
 
 def local(queries, eigenvalues, train_grads, query_index, train_index):
@@ -256,15 +282,16 @@
     half = rows // HALVES
     total = HALVES * (features // WIDTH)
     vmem = pl.BlockSpec(memory_space=pltpu.VMEM)
-    links = HALVES * (feats - 1)
+    links = HALVES * (feats - 1) * PIECES
     return pl.pallas_call(
         kernel,
         out_shape=jax.ShapeDtypeStruct((rows, local_rows), jnp.float32),
-        in_specs=[vmem, vmem, vmem, vmem, pl.BlockSpec(memory_space=pl.ANY)],
+        in_specs=[vmem, vmem, vmem] + [pl.BlockSpec(memory_space=pl.ANY)] * 2,
         out_specs=vmem,
         scratch_shapes=[
+            pltpu.VMEM((rows, features), jnp.float32),
             pltpu.VMEM((HALVES, 4 * half, features), jnp.bfloat16),
-            pltpu.VMEM((HALVES, 4 * half, local_rows), jnp.float32),
+            pltpu.VMEM((HALVES, local_rows, 4 * half), jnp.float32),
             pltpu.VMEM((local_rows, local_rows), jnp.bfloat16),
             pltpu.VMEM((KEPT, local_rows, WIDTH), jnp.bfloat16),
             pltpu.VMEM((SLOTS, local_rows, WIDTH), jnp.bfloat16),
@@ -272,11 +299,11 @@
             pltpu.VMEM((feats, HALVES, half, local_rows), jnp.bfloat16),
             pltpu.SemaphoreType.DMA((KEPT,)),
             pltpu.SemaphoreType.DMA((SLOTS,)),
-        ] + [pltpu.SemaphoreType.DMA((total,))] * 6 + [pltpu.SemaphoreType.DMA((links,))] * 2,
+        ] + [pltpu.SemaphoreType.DMA((total,))] * 6 + [pltpu.SemaphoreType.DMA((features // WIDTH,))] + [pltpu.SemaphoreType.DMA((links,))] * 2,
         compiler_params=pltpu.CompilerParams(
             collective_id=0, has_side_effects=True, vmem_limit_bytes=60 * 1024 * 1024),
         name="scores",
-    )(queries, eigenvalues.reshape(1, -1), query_index.reshape(-1, 1), train_index.reshape(1, -1), train_grads)
+    )(eigenvalues.reshape(1, -1), query_index.reshape(1, -1), train_index.reshape(1, -1), queries, train_grads)
 
 
 def solution(mesh):

time: 84.4 us -> 76.1 us (0.902)
  Pallas kernels: 80.6 us -> 74 us
  local copies, waits for them, and re-layouts: 3.23 us -> 1.87 us
    pallas_call x1, Pallas kernels: 80.6 us -> 74 us  [local(): pl.pallas_call(kernel, out_shape=jax.ShapeDtypeStruct((rows, local_rows),...]
    reshape x1 -> x0, local copies, waits for them, and re-layouts: 1.36 us -> none  [local(): query_index.reshape(-1, 1)]
where the time goes in v2:
time: 76.1 us; the launch traced here: 75.9 us
  Pallas kernels  74 us (97%)
  local copies, waits for them, and re-layouts  1.87 us (2%)
    pallas_call x1, Pallas kernels, local(): pl.pallas_call(kernel, out_shape=jax.ShapeDtypeStruct((rows, local_rows),...  74 us
    unnamed x1, local copies, waits for them, and re-layouts  1.87 us

profile of v2, /device:TPU:0, one launch (start us, length us, event | category | flops | bytes accessed | tf_op | source)
XLA Modules:
  0.0 75.9 jit_solution(15119686162468195270)
XLA Ops:
  0.0 74.0 %scores.1 = f32[64,2048]{1,0:T(8,128)} custom-call(f32[1,16384]{1,0:T(1,128)} %bitcast.3, s32[1,64]{1,0:T(1,128)} %bitcast.5, s32[1,2048]{1,0:T(1,128)} %bitcast.4, f32[64,16384]{1,0:T(8,128)} %queries_hbm.1, bf16[2048,16384]{1,0:T(8,128)(2,1)} %train.1), custom_call_target="tpu_custom_call" | custom-call | tf_op jit(solution)/shard_map/scores/pallas_call | solution.py:286
  74.0 1.9 %copy.7 = f32[64,2048]{1,0:T(8,128)} copy(f32[64,2048]{1,0:T(8,128)} %scores.1) | data formatting | bytes 1048576

commit v3 on v2

--- a/solution.py
+++ b/solution.py
@@ -120,10 +120,6 @@
         load(k).start()
     for k in range(chunks):
         load(k).wait()
-    for k in range(KEPT):
-        keep(k).start()
-    for s in range(SLOTS):
-        stream(jnp.int32(s)).start()
 
     sources = lax.broadcasted_iota(jnp.int32, (rows, rows), 0)
     pick = (query_index[...] == sources).astype(jnp.float32).astype(jnp.bfloat16)
@@ -138,6 +134,10 @@
             stack[h, mine, columns(k)] = selected[h * half:(h + 1) * half]
 
     scale(0)
+    for k in range(KEPT):
+        keep(k).start()
+    for s in range(SLOTS):
+        stream(jnp.int32(s)).start()
     pl.semaphore_wait(barrier, feats + 1)
 
     def first(k, carry):

time: 76.1 us -> 76.1 us (level)
  no operation moved by 1% of the time
where the time goes in v3:
time: 76.1 us; the launch traced here: 75.9 us
  Pallas kernels  74 us (97%)
  local copies, waits for them, and re-layouts  1.87 us (2%)
    pallas_call x1, Pallas kernels, local(): pl.pallas_call(kernel, out_shape=jax.ShapeDtypeStruct((rows, local_rows),...  74 us
    unnamed x1, local copies, waits for them, and re-layouts  1.87 us

profile of v3, /device:TPU:0, one launch (start us, length us, event | category | flops | bytes accessed | tf_op | source)
XLA Modules:
  0.0 75.9 jit_solution(15119686162468195270)
XLA Ops:
  0.0 74.0 %scores.1 = f32[64,2048]{1,0:T(8,128)} custom-call(f32[1,16384]{1,0:T(1,128)} %bitcast.3, s32[1,64]{1,0:T(1,128)} %bitcast.5, s32[1,2048]{1,0:T(1,128)} %bitcast.4, f32[64,16384]{1,0:T(8,128)} %queries_hbm.1, bf16[2048,16384]{1,0:T(8,128)(2,1)} %train.1), custom_call_target="tpu_custom_call" | custom-call | tf_op jit(solution)/shard_map/scores/pallas_call | solution.py:286
  74.0 1.9 %copy.7 = f32[64,2048]{1,0:T(8,128)} copy(f32[64,2048]{1,0:T(8,128)} %scores.1) | data formatting | bytes 1048576
